TPU v7x, 32 devices: a whole 2x2x4 slice. The times are simulated.
32 devices in a mesh: mem: 8 (over z, core), reg: 4 (over y, x).
Axes of the slice: x: 2, y: 2, z: 4, core: 2. Of those that a mesh axis runs over, the one named last changes fastest.
Arguments:
- anomalies: bfloat16 [1024, 65536], P('mem', 'reg'), may hold values from -6 to 6
- obs_anomalies: bfloat16 [1024, 2048], P('mem', 'reg'), may hold values from -6 to 6
- innovations: bfloat16 [1024, 2048], P('mem', 'reg'), may hold values from -6 to 6
- obs_links: int32 [512, 12], P('reg'), may hold values from 0 to 19, as said below
- taper_choice: int32 [512, 12], P('reg'), may hold values from 0 to 7
- tapers: float32 [8, 128, 128], replicated, may hold values from 0.1 to 1
Outputs:
- increments: bfloat16 [1024, 65536], P('mem', 'reg')
Inputs may be any that keep to these rules, and one draw needn't show every extreme that they name: `obs_links`: each row names 12 different positions of a window of 20 observation blocks: position w is block w mod 4 of region r + w // 4 - 2 (regions counted cyclically), r being the state block's region.
All inputs are finite; a program needn't handle non-finite values.
Results may differ from a plain program's by a relative error of at most 0.005.
Values may be sent and summed in bfloat16 or wider, within the bound.
A program may use at most 128 MiB of HBM per device.

v0:
```python
import jax
import jax.numpy as jnp
from jax import lax
from jax.sharding import PartitionSpec as P

BLK = 128


def from_behind(x, axis, by):
    size = lax.axis_size(axis)
    return lax.ppermute(x, axis, [(i, (i + by) % size) for i in range(size)])


def neighbour_window(stacked):
    pieces = []
    for distance in (2, 1, 0, -1, -2):
        if distance == 0:
            pieces.append(stacked)
        else:
            pieces.append(from_behind(stacked, "reg", distance))
    return jnp.concatenate(pieces, axis=2)


def local(anomalies, obs_anomalies, innovations, obs_links, taper_choice, tapers):
    mem_dev, state_cols = anomalies.shape
    mem_count = lax.axis_size("mem")
    members = mem_dev * mem_count
    per_dev = state_cols // BLK // mem_count
    member_major = anomalies.reshape(mem_dev, mem_count, per_dev * BLK)
    patches = lax.all_to_all(member_major, "mem", split_axis=1, concat_axis=0, tiled=True).reshape(
        members, per_dev * BLK
    )
    stacked = jnp.stack([obs_anomalies, innovations])
    window = neighbour_window(lax.all_gather(stacked, "mem", axis=1, tiled=True))
    window_obs = window[0]
    window_innov = window[1]
    window_cols = window_obs.shape[1]
    window_blocks = window_cols // BLK
    first_block = lax.axis_index("mem") * per_dev
    my_links = lax.dynamic_slice_in_dim(obs_links, first_block, per_dev, 0)
    my_tapers = lax.dynamic_slice_in_dim(taper_choice, first_block, per_dev, 0)
    position_ids = jnp.arange(window_blocks, dtype=jnp.int32)
    taper_ids = jnp.arange(tapers.shape[0], dtype=jnp.int32)

    def advance(position, result_cols):
        state_block = lax.dynamic_slice_in_dim(patches, position * BLK, BLK, 1)
        link_row = lax.dynamic_index_in_dim(my_links, position, 0, keepdims=False)
        taper_row = lax.dynamic_index_in_dim(my_tapers, position, 0, keepdims=False)
        link_onehot = (link_row[:, None] == position_ids[None, :]).astype(jnp.float32)
        taper_onehot = (taper_row[:, None] == taper_ids[None, :]).astype(jnp.float32)
        weights = jnp.dot(
            link_onehot.T,
            taper_onehot,
            precision=lax.Precision.HIGHEST,
            preferred_element_type=jnp.float32,
        )
        taper_tile = jnp.einsum(
            "wt,tij->iwj", weights, tapers, precision=lax.Precision.HIGHEST
        ).reshape(BLK, window_cols)
        covariance = lax.dot_general(
            state_block, window_obs, (((0,), (0,)), ((), ())), preferred_element_type=jnp.float32
        ) / (members - 1)
        tapered = (covariance * taper_tile).astype(jnp.bfloat16)
        increment = lax.dot_general(
            window_innov, tapered, (((1,), (1,)), ((), ())), preferred_element_type=jnp.float32
        ).astype(jnp.bfloat16)
        return lax.dynamic_update_slice_in_dim(result_cols, increment, position * BLK, 1)

    result_cols = lax.fori_loop(
        0, per_dev, advance, jnp.zeros((members, per_dev * BLK), jnp.bfloat16)
    )
    returned = lax.all_to_all(
        result_cols.reshape(members, 1, per_dev * BLK),
        "mem",
        split_axis=0,
        concat_axis=1,
        tiled=True,
    )
    return returned.reshape(mem_dev, state_cols)


def solution(mesh):
    return jax.shard_map(
        local,
        mesh=mesh,
        in_specs=(
            P("mem", "reg"),
            P("mem", "reg"),
            P("mem", "reg"),
            P("reg", None),
            P("reg", None),
            P(),
        ),
        out_specs=P("mem", "reg"),
        check_vma=False,
    )
```

profile of v0, /device:TPU:1, one launch (start us, length us, event | category | flops | bytes accessed | tf_op | source)
XLA Modules:
  0.0 497.9 jit_solution(7605965444030726110)
XLA Ops:
  19.6 37.3 %all-gather.2.cloned.1.call-done = bf16[2,1024,512]{2,1,0:T(8,128)(2,1)} async-done(((bf16[2,128,512]{2,1,0:T(8,128)(2,1)}), bf16[2,1024,512]{2,1,0:T(8,128)(2,1)}) %all-gather.2.cloned.1.call-update) | async-done | bytes 2097168 | tf_op jit(solution)/shard_map/all_gather | solution.py:34
  60.8 88.2 %collective-permute-done = bf16[2,1024,512]{2,1,0:T(8,128)(2,1)S(1)} collective-permute-done((bf16[2,1024,512]{2,1,0:T(8,128)(2,1)}, bf16[2,1024,512]{2,1,0:T(8,128)(2,1)S(1)}, u32[]{:S(2)}, u32[]{:S(2)}) %collective-permute-start) | collective-permute-done | bytes 2097184 | tf_op jit(solution)/shard_map/ppermute | solution.py:11
  160.1 8.6 %slice_bitcast_fusion = (bf16[1024,2560]{1,0:T(8,128)(2,1)}, bf16[1024,2560]{1,0:T(8,128)(2,1)}) fusion(bf16[2,1024,2560]{2,1,0:T(8,128)(2,1)} %constant_dynamic-update-slice_fusion), kind=kLoop, calls=%fused_computation.22 | loop fusion | bytes 20971520 | tf_op jit(solution)/shard_map/squeeze | solution.py:36
  171.2 159.4 %while.14 = (s32[]{:T(128)}, bf16[1024,2048]{0,1:T(8,128)(2,1)}, bf16[1024,2048]{1,0:T(8,128)(2,1)}, bf16[1024,2560]{1,0:T(8,128)(2,1)}, s32[16,12]{1,0:T(8,128)...) while((s32[]{:T(128)}, bf16[1024,2048]{0,1:T(8,128)(2,1)}, ...), condition=%wide.region_1.2_spmd.clone, body=%wide.region_0.1_spmd.clone.sunk | while | flops 1374752896 | bytes 19401416 | solution.py:69
  173.8 7.4 %fusion.35 = bf16[1024,2048]{0,1:T(8,128)(2,1)} fusion(bf16[1024,2048]{0,1:T(8,128)(2,1)} %get-tuple-element.322, s32[]{:T(128)S(6)} %select_n.22, bf16[1024,2560]{1,0:T(8,128)(2,1)} %get-tuple-element.340, f32[128,2560]{1,0:T(8,128)S(1)} %copy.56, bf16[1024,2560]{1,0:T(8,128)(2,1)} %get-tuple-element.336, bf16[1024,2048]{1,0:T(8,128)(2,1)} %get-tuple-element.335), kind=kOutput, calls=%fused_computation.8.clone.1 | convolution fusion | flops 1343291392 | bytes 12321792 | tf_op jit(solution)/shard_map/while/body/eval_jaxpr/dot_general | solution.py:64
  183.7 7.4 %fusion.35 = bf16[1024,2048]{0,1:T(8,128)(2,1)} fusion(bf16[1024,2048]{0,1:T(8,128)(2,1)} %get-tuple-element.322, s32[]{:T(128)S(6)} %select_n.22, bf16[1024,2560]{1,0:T(8,128)(2,1)} %get-tuple-element.340, f32[128,2560]{1,0:T(8,128)S(1)} %copy.56, bf16[1024,2560]{1,0:T(8,128)(2,1)} %get-tuple-element.336, bf16[1024,2048]{1,0:T(8,128)(2,1)} %get-tuple-element.335), kind=kOutput, calls=%fused_computation.8.clone.1 | convolution fusion | flops 1343291392 | bytes 12321792 | tf_op jit(solution)/shard_map/while/body/eval_jaxpr/dot_general | solution.py:64
  193.7 7.4 %fusion.35 = bf16[1024,2048]{0,1:T(8,128)(2,1)} fusion(bf16[1024,2048]{0,1:T(8,128)(2,1)} %get-tuple-element.322, s32[]{:T(128)S(6)} %select_n.22, bf16[1024,2560]{1,0:T(8,128)(2,1)} %get-tuple-element.340, f32[128,2560]{1,0:T(8,128)S(1)} %copy.56, bf16[1024,2560]{1,0:T(8,128)(2,1)} %get-tuple-element.336, bf16[1024,2048]{1,0:T(8,128)(2,1)} %get-tuple-element.335), kind=kOutput, calls=%fused_computation.8.clone.1 | convolution fusion | flops 1343291392 | bytes 12321792 | tf_op jit(solution)/shard_map/while/body/eval_jaxpr/dot_general | solution.py:64
  203.7 7.4 %fusion.35 = bf16[1024,2048]{0,1:T(8,128)(2,1)} fusion(bf16[1024,2048]{0,1:T(8,128)(2,1)} %get-tuple-element.322, s32[]{:T(128)S(6)} %select_n.22, bf16[1024,2560]{1,0:T(8,128)(2,1)} %get-tuple-element.340, f32[128,2560]{1,0:T(8,128)S(1)} %copy.56, bf16[1024,2560]{1,0:T(8,128)(2,1)} %get-tuple-element.336, bf16[1024,2048]{1,0:T(8,128)(2,1)} %get-tuple-element.335), kind=kOutput, calls=%fused_computation.8.clone.1 | convolution fusion | flops 1343291392 | bytes 12321792 | tf_op jit(solution)/shard_map/while/body/eval_jaxpr/dot_general | solution.py:64
  213.6 7.4 %fusion.35 = bf16[1024,2048]{0,1:T(8,128)(2,1)} fusion(bf16[1024,2048]{0,1:T(8,128)(2,1)} %get-tuple-element.322, s32[]{:T(128)S(6)} %select_n.22, bf16[1024,2560]{1,0:T(8,128)(2,1)} %get-tuple-element.340, f32[128,2560]{1,0:T(8,128)S(1)} %copy.56, bf16[1024,2560]{1,0:T(8,128)(2,1)} %get-tuple-element.336, bf16[1024,2048]{1,0:T(8,128)(2,1)} %get-tuple-element.335), kind=kOutput, calls=%fused_computation.8.clone.1 | convolution fusion | flops 1343291392 | bytes 12321792 | tf_op jit(solution)/shard_map/while/body/eval_jaxpr/dot_general | solution.py:64
  223.6 7.4 %fusion.35 = bf16[1024,2048]{0,1:T(8,128)(2,1)} fusion(bf16[1024,2048]{0,1:T(8,128)(2,1)} %get-tuple-element.322, s32[]{:T(128)S(6)} %select_n.22, bf16[1024,2560]{1,0:T(8,128)(2,1)} %get-tuple-element.340, f32[128,2560]{1,0:T(8,128)S(1)} %copy.56, bf16[1024,2560]{1,0:T(8,128)(2,1)} %get-tuple-element.336, bf16[1024,2048]{1,0:T(8,128)(2,1)} %get-tuple-element.335), kind=kOutput, calls=%fused_computation.8.clone.1 | convolution fusion | flops 1343291392 | bytes 12321792 | tf_op jit(solution)/shard_map/while/body/eval_jaxpr/dot_general | solution.py:64
  233.5 7.4 %fusion.35 = bf16[1024,2048]{0,1:T(8,128)(2,1)} fusion(bf16[1024,2048]{0,1:T(8,128)(2,1)} %get-tuple-element.322, s32[]{:T(128)S(6)} %select_n.22, bf16[1024,2560]{1,0:T(8,128)(2,1)} %get-tuple-element.340, f32[128,2560]{1,0:T(8,128)S(1)} %copy.56, bf16[1024,2560]{1,0:T(8,128)(2,1)} %get-tuple-element.336, bf16[1024,2048]{1,0:T(8,128)(2,1)} %get-tuple-element.335), kind=kOutput, calls=%fused_computation.8.clone.1 | convolution fusion | flops 1343291392 | bytes 12321792 | tf_op jit(solution)/shard_map/while/body/eval_jaxpr/dot_general | solution.py:64
  243.5 7.4 %fusion.35 = bf16[1024,2048]{0,1:T(8,128)(2,1)} fusion(bf16[1024,2048]{0,1:T(8,128)(2,1)} %get-tuple-element.322, s32[]{:T(128)S(6)} %select_n.22, bf16[1024,2560]{1,0:T(8,128)(2,1)} %get-tuple-element.340, f32[128,2560]{1,0:T(8,128)S(1)} %copy.56, bf16[1024,2560]{1,0:T(8,128)(2,1)} %get-tuple-element.336, bf16[1024,2048]{1,0:T(8,128)(2,1)} %get-tuple-element.335), kind=kOutput, calls=%fused_computation.8.clone.1 | convolution fusion | flops 1343291392 | bytes 12321792 | tf_op jit(solution)/shard_map/while/body/eval_jaxpr/dot_general | solution.py:64
  253.5 7.4 %fusion.35 = bf16[1024,2048]{0,1:T(8,128)(2,1)} fusion(bf16[1024,2048]{0,1:T(8,128)(2,1)} %get-tuple-element.322, s32[]{:T(128)S(6)} %select_n.22, bf16[1024,2560]{1,0:T(8,128)(2,1)} %get-tuple-element.340, f32[128,2560]{1,0:T(8,128)S(1)} %copy.56, bf16[1024,2560]{1,0:T(8,128)(2,1)} %get-tuple-element.336, bf16[1024,2048]{1,0:T(8,128)(2,1)} %get-tuple-element.335), kind=kOutput, calls=%fused_computation.8.clone.1 | convolution fusion | flops 1343291392 | bytes 12321792 | tf_op jit(solution)/shard_map/while/body/eval_jaxpr/dot_general | solution.py:64
  263.4 7.4 %fusion.35 = bf16[1024,2048]{0,1:T(8,128)(2,1)} fusion(bf16[1024,2048]{0,1:T(8,128)(2,1)} %get-tuple-element.322, s32[]{:T(128)S(6)} %select_n.22, bf16[1024,2560]{1,0:T(8,128)(2,1)} %get-tuple-element.340, f32[128,2560]{1,0:T(8,128)S(1)} %copy.56, bf16[1024,2560]{1,0:T(8,128)(2,1)} %get-tuple-element.336, bf16[1024,2048]{1,0:T(8,128)(2,1)} %get-tuple-element.335), kind=kOutput, calls=%fused_computation.8.clone.1 | convolution fusion | flops 1343291392 | bytes 12321792 | tf_op jit(solution)/shard_map/while/body/eval_jaxpr/dot_general | solution.py:64
  273.4 7.4 %fusion.35 = bf16[1024,2048]{0,1:T(8,128)(2,1)} fusion(bf16[1024,2048]{0,1:T(8,128)(2,1)} %get-tuple-element.322, s32[]{:T(128)S(6)} %select_n.22, bf16[1024,2560]{1,0:T(8,128)(2,1)} %get-tuple-element.340, f32[128,2560]{1,0:T(8,128)S(1)} %copy.56, bf16[1024,2560]{1,0:T(8,128)(2,1)} %get-tuple-element.336, bf16[1024,2048]{1,0:T(8,128)(2,1)} %get-tuple-element.335), kind=kOutput, calls=%fused_computation.8.clone.1 | convolution fusion | flops 1343291392 | bytes 12321792 | tf_op jit(solution)/shard_map/while/body/eval_jaxpr/dot_general | solution.py:64
  283.4 7.4 %fusion.35 = bf16[1024,2048]{0,1:T(8,128)(2,1)} fusion(bf16[1024,2048]{0,1:T(8,128)(2,1)} %get-tuple-element.322, s32[]{:T(128)S(6)} %select_n.22, bf16[1024,2560]{1,0:T(8,128)(2,1)} %get-tuple-element.340, f32[128,2560]{1,0:T(8,128)S(1)} %copy.56, bf16[1024,2560]{1,0:T(8,128)(2,1)} %get-tuple-element.336, bf16[1024,2048]{1,0:T(8,128)(2,1)} %get-tuple-element.335), kind=kOutput, calls=%fused_computation.8.clone.1 | convolution fusion | flops 1343291392 | bytes 12321792 | tf_op jit(solution)/shard_map/while/body/eval_jaxpr/dot_general | solution.py:64
  293.3 7.4 %fusion.35 = bf16[1024,2048]{0,1:T(8,128)(2,1)} fusion(bf16[1024,2048]{0,1:T(8,128)(2,1)} %get-tuple-element.322, s32[]{:T(128)S(6)} %select_n.22, bf16[1024,2560]{1,0:T(8,128)(2,1)} %get-tuple-element.340, f32[128,2560]{1,0:T(8,128)S(1)} %copy.56, bf16[1024,2560]{1,0:T(8,128)(2,1)} %get-tuple-element.336, bf16[1024,2048]{1,0:T(8,128)(2,1)} %get-tuple-element.335), kind=kOutput, calls=%fused_computation.8.clone.1 | convolution fusion | flops 1343291392 | bytes 12321792 | tf_op jit(solution)/shard_map/while/body/eval_jaxpr/dot_general | solution.py:64
  303.3 7.4 %fusion.35 = bf16[1024,2048]{0,1:T(8,128)(2,1)} fusion(bf16[1024,2048]{0,1:T(8,128)(2,1)} %get-tuple-element.322, s32[]{:T(128)S(6)} %select_n.22, bf16[1024,2560]{1,0:T(8,128)(2,1)} %get-tuple-element.340, f32[128,2560]{1,0:T(8,128)S(1)} %copy.56, bf16[1024,2560]{1,0:T(8,128)(2,1)} %get-tuple-element.336, bf16[1024,2048]{1,0:T(8,128)(2,1)} %get-tuple-element.335), kind=kOutput, calls=%fused_computation.8.clone.1 | convolution fusion | flops 1343291392 | bytes 12321792 | tf_op jit(solution)/shard_map/while/body/eval_jaxpr/dot_general | solution.py:64
  313.2 7.4 %fusion.35 = bf16[1024,2048]{0,1:T(8,128)(2,1)} fusion(bf16[1024,2048]{0,1:T(8,128)(2,1)} %get-tuple-element.322, s32[]{:T(128)S(6)} %select_n.22, bf16[1024,2560]{1,0:T(8,128)(2,1)} %get-tuple-element.340, f32[128,2560]{1,0:T(8,128)S(1)} %copy.56, bf16[1024,2560]{1,0:T(8,128)(2,1)} %get-tuple-element.336, bf16[1024,2048]{1,0:T(8,128)(2,1)} %get-tuple-element.335), kind=kOutput, calls=%fused_computation.8.clone.1 | convolution fusion | flops 1343291392 | bytes 12321792 | tf_op jit(solution)/shard_map/while/body/eval_jaxpr/dot_general | solution.py:64
  323.2 7.4 %fusion.35 = bf16[1024,2048]{0,1:T(8,128)(2,1)} fusion(bf16[1024,2048]{0,1:T(8,128)(2,1)} %get-tuple-element.322, s32[]{:T(128)S(6)} %select_n.22, bf16[1024,2560]{1,0:T(8,128)(2,1)} %get-tuple-element.340, f32[128,2560]{1,0:T(8,128)S(1)} %copy.56, bf16[1024,2560]{1,0:T(8,128)(2,1)} %get-tuple-element.336, bf16[1024,2048]{1,0:T(8,128)(2,1)} %get-tuple-element.335), kind=kOutput, calls=%fused_computation.8.clone.1 | convolution fusion | flops 1343291392 | bytes 12321792 | tf_op jit(solution)/shard_map/while/body/eval_jaxpr/dot_general | solution.py:64
  345.0 7.8 %reshape.33 = bf16[8,2,131072]{2,1,0:T(2,128)(2,1)} reshape(bf16[1024,2048]{1,0:T(8,128)(2,1)} %copy.52) | data formatting | bytes 8388608
  352.8 108.7 %all_to_all.30 = bf16[8,2,131072]{2,1,0:T(2,128)(2,1)} all-to-all(bf16[8,2,131072]{2,1,0:T(2,128)(2,1)} %reshape.33), channel_id=1, replica_groups=mesh['mem'=8,'reg'=4] {'mem'}, dimensions={0} | all-to-all | bytes 8388608 | tf_op jit(solution)/shard_map/all_to_all | solution.py:72
  461.5 8.8 %reshape.34 = bf16[1024,1,2048]{2,1,0:T(2,128)(2,1)} reshape(bf16[8,2,131072]{2,1,0:T(2,128)(2,1)} %all_to_all.30) | data formatting | bytes 8388608
  470.2 8.0 %copy.46 = bf16[1024,1,2048]{2,0,1:T(8,128)(2,1)} copy(bf16[1024,1,2048]{2,1,0:T(2,128)(2,1)} %reshape.34) | data formatting | bytes 8388608
  (114 shorter events, 98.0 us)
Async XLA Ops:
  6.5 50.3 %all-gather.2.cloned.1.call-start = ((), (), s32[]{:S(2)}) async-start(), calls=%async_computation.2 | async-start | bytes 2359296 | tf_op jit(solution)/shard_map/all_gather | solution.py:34
  13.1 47.2 %copy-start.2 = (s32[128,12]{0,1:T(8,128)S(1)}, s32[128,12]{0,1:T(8,128)}, u32[]{:S(2)}) copy-start(s32[128,12]{0,1:T(8,128)} %param.12) | copy-start | bytes 18436
  13.1 47.2 %copy-start.3 = (s32[128,12]{0,1:T(8,128)S(1)}, s32[128,12]{0,1:T(8,128)}, u32[]{:S(2)}) copy-start(s32[128,12]{0,1:T(8,128)} %param.11) | copy-start | bytes 18436
  13.1 47.5 %copy-start.1 = (f32[8,128,128]{2,1,0:T(8,128)S(1)}, f32[8,128,128]{2,1,0:T(8,128)}, u32[]{:S(2)}) copy-start(f32[8,128,128]{2,1,0:T(8,128)} %param.13) | copy-start | bytes 1572868
  13.1 155.6 %all-to-all-start = ((bf16[128,8,2048]{2,0,1:T(8,128)(2,1)}), bf16[128,8,2048]{2,0,1:T(8,128)(2,1)}, u32[]{:S(2)}, u32[]{:S(2)}) async-start(bf16[128,8,2048]{2,0,1:T(8,128)(2,1)} %bitcast.57), calls=%async_computation | async-start | bytes 8388608 | tf_op jit(solution)/shard_map/all_to_all | solution.py:30
  56.8 92.2 %collective-permute-start = (bf16[2,1024,512]{2,1,0:T(8,128)(2,1)}, bf16[2,1024,512]{2,1,0:T(8,128)(2,1)S(1)}, u32[]{:S(2)}, u32[]{:S(2)}) collective-permute-start(bf16[2,1024,512]{2,1,0:T(8,128)(2,1)} %all-gather.2.cloned.1.call-done), channel_id=1, source_target_pairs={{0,2},{1,3},{2,0},{3,1},{4,6},{5,7},{6,4},{7,5},{8,10},{9,11},{10,... | collective-permute-start | bytes 6291464 | tf_op jit(solution)/shard_map/ppermute | solution.py:11
  57.9 92.8 %collective-permute-start.1 = (bf16[2,1024,512]{2,1,0:T(8,128)(2,1)}, bf16[2,1024,512]{2,1,0:T(8,128)(2,1)}, u32[]{:S(2)}, u32[]{:S(2)}) collective-permute-start(bf16[2,1024,512]{2,1,0:T(8,128)(2,1)} %all-gather.2.cloned.1.call-done), channel_id=1, source_target_pairs={{0,1},{1,2},{2,3},{3,0},{4,5},{5,6},{6,7},{7,4},{8,9},{9,10},{10,1... | collective-permute-start | bytes 6291464 | tf_op jit(solution)/shard_map/ppermute | solution.py:11
  59.1 96.4 %collective-permute-start.2 = (bf16[2,1024,512]{2,1,0:T(8,128)(2,1)}, bf16[2,1024,512]{2,1,0:T(8,128)(2,1)}, u32[]{:S(2)}, u32[]{:S(2)}) collective-permute-start(bf16[2,1024,512]{2,1,0:T(8,128)(2,1)} %all-gather.2.cloned.1.call-done), channel_id=1, source_target_pairs={{0,3},{1,0},{2,1},{3,2},{4,7},{5,4},{6,5},{7,6},{8,11},{9,8},{10,9... | collective-permute-start | bytes 6291464 | tf_op jit(solution)/shard_map/ppermute | solution.py:11
  60.8 93.0 %copy-start = (bf16[2,1024,512]{2,1,0:T(8,128)(2,1)S(1)}, bf16[2,1024,512]{2,1,0:T(8,128)(2,1)}, u32[]{:S(2)}) copy-start(bf16[2,1024,512]{2,1,0:T(8,128)(2,1)} %all-gather.2.cloned.1.call-done) | copy-start | bytes 6291460
Sparse Core Ops, SparseCore 0:
  9.0 47.8 all-gather.1
where the time goes:
time: 500 us; the launch traced here: 498 us
  matrix products  146 us (29%)
  waiting for transfers between devices  126 us (25%)
  blocking collectives  109 us (22%)
  local copies, waits for them, and re-layouts  85.3 us (17%)
  between operations  13.4 us (3%)
  starting transfers between devices  9.94 us (2%)
  other arithmetic  9.03 us (2%)
    dot_general x16, matrix products, advance(): lax.dot_general(window_innov, tapered, (((1,), (1,)), ((), ())), preferre...  119 us
    all_to_all x1, blocking collectives, local(): lax.all_to_all(result_cols.reshape(members, 1, per_dev * BLK), 'mem', spl...  109 us
    ppermute x3, waiting for transfers between devices, from_behind(): return lax.ppermute(x, axis, [(i, (i + by) % size) for i in range(size)])  88.2 us
    unnamed x19, local copies, waits for them, and re-layouts  41 us
    all_gather x1, waiting for transfers between devices, local(): lax.all_gather(stacked, 'mem', axis=1, tiled=True)  37.3 us
    dot_general x16, matrix products, advance(): jnp.einsum('wt,tij->iwj', weights, tapers, precision=lax.Precision.HIGHEST)  22.8 us
  transfers between devices with their start and end apart: 5, of which 2 were waited for; matrix products, arithmetic and copies ran while one was open for 5% of the time, Pallas kernels for 0%

commit v1 on v0

v1 whole, which is shorter than its diff:
```python
import functools

import jax
import jax.numpy as jnp
from jax import lax
from jax.experimental import pallas as pl
from jax.experimental.pallas import tpu as pltpu
from jax.sharding import PartitionSpec as P

BLK = 128
REACH = 2
CORES = 2
MESH = pl.DeviceIdType.MESH


def wait_for(ref, sem):
    pltpu.make_async_copy(ref, ref, sem).wait()


def kernel(
    mem_count,
    reg_count,
    chunk,
    slots,
    steps,
    index_ref,
    taper_ref,
    anomalies,
    obs,
    innov,
    out,
    patches,
    window,
    turned,
    weighted,
    results,
    patch_send,
    patch_recv,
    out_send,
    out_recv,
    line_send,
    line_recv,
    pair_send,
    pair_recv,
    plane_send,
    plane_recv,
):
    mem = lax.axis_index("mem")
    reg = lax.axis_index("reg")
    chips = mem_count // CORES
    chip = mem // CORES
    core = lax.rem(mem, CORES)
    twin = chip * CORES + (1 - core)
    mem_dev = anomalies.shape[0]
    chunks = patches.shape[0]
    own_cols = chunks * chunk
    groups = window.shape[5] // BLK
    home = REACH % reg_count
    mem_order = sorted(range(1, mem_count), key=lambda by: abs(by - mem_count // 2))
    mine = pl.ds(pl.multiple_of(mem * mem_dev, mem_dev), mem_dev)

    def device(by):
        return lax.rem(mem + by, mem_count)

    def region(step):
        return lax.rem(reg + step + reg_count, reg_count)

    barrier = pltpu.get_barrier_semaphore()
    for by in range(1, mem_count):
        pl.semaphore_signal(barrier, inc=1, device_id=(device(by), reg), device_id_type=MESH)
    for step in steps:
        pl.semaphore_signal(barrier, inc=1, device_id=(mem, region(step)), device_id_type=MESH)
    pl.semaphore_wait(barrier, mem_count - 1 + len(steps))

    for kind, shard in ((0, obs), (1, innov)):
        there = window.at[home, kind, chip, core]
        for by in range(1, chips):
            peer = lax.rem(chip + by, chips) * CORES + core
            pltpu.make_async_remote_copy(
                shard, there, line_send, line_recv, device_id=(peer, reg), device_id_type=MESH
            ).start()
        pltpu.make_async_copy(shard, there, line_recv).start()

    def send_patches(c, carry):
        there = patches.at[c, mine]
        for by in mem_order:
            peer = device(by)
            first = pl.multiple_of(peer * own_cols + c * chunk, chunk)
            pltpu.make_async_remote_copy(
                anomalies.at[:, pl.ds(first, chunk)],
                there,
                patch_send,
                patch_recv.at[c],
                device_id=(peer, reg),
                device_id_type=MESH,
            ).start()
        first = pl.multiple_of(mem * own_cols + c * chunk, chunk)
        pltpu.make_async_copy(anomalies.at[:, pl.ds(first, chunk)], there, patch_recv.at[c]).start()
        return carry

    early = max(1, chunks // 8)
    middle = max(early, chunks * 5 // 8)
    lax.fori_loop(0, early, send_patches, 0)

    def share(slot):
        return window.at[slot, :, :, core]

    def other(slot):
        return window.at[slot, :, :, 1 - core]

    def to_twin(slot):
        pltpu.make_async_remote_copy(
            share(slot),
            share(slot),
            pair_send.at[slot],
            pair_recv.at[slot],
            device_id=(twin, reg),
            device_id_type=MESH,
        ).start()

    wait_for(share(home), line_recv)
    for step in steps:
        slot = (REACH - step) % reg_count
        pltpu.make_async_remote_copy(
            share(home),
            share(slot),
            plane_send.at[slot],
            plane_recv.at[slot],
            device_id=(mem, region(step)),
            device_id_type=MESH,
        ).start()
    to_twin(home)
    lax.fori_loop(early, middle, send_patches, 0)
    for step in steps:
        slot = (REACH - step) % reg_count
        wait_for(share(slot), plane_recv.at[slot])
        to_twin(slot)
    lax.fori_loop(middle, chunks, send_patches, 0)
    for slot in range(slots):
        wait_for(other(slot), pair_recv.at[slot])

    members = mem_count * mem_dev
    rows = min(256, members)
    positions = (2 * REACH + 1) * groups

    def analyse(c, carry):
        wait_for(patches.at[c], patch_recv.at[c])
        turned[...] = patches[c].T
        for slot in range(slots):
            cov = jnp.dot(
                turned[...],
                window[slot, 0].reshape(members, groups * BLK),
                preferred_element_type=jnp.float32,
            )
            for part in range(chunk // BLK):
                for group in range(groups):
                    tile = None
                    for w in range(slot * groups + group, positions, reg_count * groups):
                        one = taper_ref[index_ref[c * (chunk // BLK) + part, w]]
                        tile = one if tile is None else tile + one
                    piece = cov[part * BLK : (part + 1) * BLK, group * BLK : (group + 1) * BLK]
                    weighted[
                        slot, part * BLK : (part + 1) * BLK, group * BLK : (group + 1) * BLK
                    ] = (piece * tile).astype(jnp.bfloat16)
        flat = [window.at[slot, 1] for slot in range(slots)]
        per_chip = CORES * mem_dev
        for k in range(chips):
            total = None
            for slot in range(slots):
                term = lax.dot_general(
                    flat[slot][k].reshape(per_chip, groups * BLK),
                    weighted[slot],
                    (((1,), (1,)), ((), ())),
                    preferred_element_type=jnp.float32,
                )
                total = term if total is None else total + term
            results[c, k * per_chip : (k + 1) * per_chip, :] = total.astype(jnp.bfloat16)
        there = out.at[:, pl.ds(pl.multiple_of(mem * own_cols + c * chunk, chunk), chunk)]
        for by in mem_order:
            peer = device(by)
            pltpu.make_async_remote_copy(
                results.at[c, pl.ds(pl.multiple_of(peer * mem_dev, mem_dev), mem_dev)],
                there,
                out_send,
                out_recv,
                device_id=(peer, reg),
                device_id_type=MESH,
            ).start()
        pltpu.make_async_copy(results.at[c, mine], there, out_recv).start()
        return carry

    lax.fori_loop(0, chunks, analyse, 0)

    wait_for(out, out_recv)
    sent = pl.ds(0, (mem_count - 1) * own_cols)
    wait_for(anomalies.at[:, sent], patch_send)
    wait_for(out.at[:, sent], out_send)
    wait_for(window.at[home, :, 0 : chips - 1, 0], line_send)
    for slot in range(slots):
        wait_for(share(slot), pair_send.at[slot])
        if slot != home:
            wait_for(share(home), plane_send.at[slot])


def local(anomalies, obs_anomalies, innovations, obs_links, taper_choice, tapers):
    mem_dev, state_cols = anomalies.shape
    mem_count = lax.axis_size("mem")
    reg_count = lax.axis_size("reg")
    members = mem_dev * mem_count
    per_dev = state_cols // BLK // mem_count
    pair = 2 if per_dev % 2 == 0 else 1
    chunk = pair * BLK
    chunks = per_dev // pair
    obs_cols = obs_anomalies.shape[1]
    positions = (2 * REACH + 1) * obs_cols // BLK
    slots = min(2 * REACH + 1, reg_count)
    home = REACH % reg_count
    steps = [(REACH - slot) for slot in range(slots) if slot != home]
    first_block = lax.axis_index("mem") * per_dev
    my_links = lax.dynamic_slice_in_dim(obs_links, first_block, per_dev, 0)
    my_choice = lax.dynamic_slice_in_dim(taper_choice, first_block, per_dev, 0)
    position_ids = jnp.arange(positions, dtype=jnp.int32)
    linked = my_links[:, :, None] == position_ids[None, None, :]
    index = jnp.sum(jnp.where(linked, my_choice[:, :, None] + 1, 0), axis=1).astype(jnp.int32)
    tiles = jnp.concatenate([jnp.zeros((1, BLK, BLK), jnp.float32), tapers]) / (members - 1)
    DMA = pltpu.SemaphoreType.DMA
    chips = mem_count // CORES
    return pl.pallas_call(
        functools.partial(kernel, mem_count, reg_count, chunk, slots, steps),
        out_shape=jax.ShapeDtypeStruct((mem_dev, state_cols), jnp.bfloat16),
        in_specs=[
            pl.BlockSpec(memory_space=pltpu.SMEM),
            pl.BlockSpec(memory_space=pltpu.VMEM),
            pl.BlockSpec(memory_space=pl.ANY),
            pl.BlockSpec(memory_space=pl.ANY),
            pl.BlockSpec(memory_space=pl.ANY),
        ],
        out_specs=pl.BlockSpec(memory_space=pl.ANY),
        scratch_shapes=[
            pltpu.VMEM((chunks, members, chunk), jnp.bfloat16),
            pltpu.VMEM((slots, 2, chips, CORES, mem_dev, obs_cols), jnp.bfloat16),
            pltpu.VMEM((chunk, members), jnp.bfloat16),
            pltpu.VMEM((slots, chunk, obs_cols), jnp.bfloat16),
            pltpu.VMEM((chunks, members, chunk), jnp.bfloat16),
            DMA,
            DMA((chunks,)),
            DMA,
            DMA,
            DMA,
            DMA,
            DMA((slots,)),
            DMA((slots,)),
            DMA((slots,)),
            DMA((slots,)),
        ],
        compiler_params=pltpu.CompilerParams(
            collective_id=0, has_side_effects=True, vmem_limit_bytes=48 * 1024 * 1024
        ),
        cost_estimate=pl.CostEstimate(
            flops=4 * members * per_dev * BLK * slots * obs_cols,
            bytes_accessed=4 * mem_dev * state_cols * 2,
            transcendentals=0,
        ),
    )(index, tiles, anomalies, obs_anomalies, innovations)


def solution(mesh):
    return jax.shard_map(
        local,
        mesh=mesh,
        in_specs=(
            P("mem", "reg"),
            P("mem", "reg"),
            P("mem", "reg"),
            P("reg", None),
            P("reg", None),
            P(),
        ),
        out_specs=P("mem", "reg"),
        check_vma=False,
    )
```

time: 500 us -> 214 us (0.43)
  Pallas kernels: 0 us -> 208 us
  matrix products: 146 us -> 0 us
  waiting for transfers between devices: 126 us -> 0 us
  blocking collectives: 109 us -> 0 us
  local copies, waits for them, and re-layouts: 85.3 us -> 3.82 us
  between operations: 13.4 us -> 0.03 us
  starting transfers between devices: 9.94 us -> 0 us
  other arithmetic: 9.03 us -> 1.99 us
    pallas_call x0 -> x1, Pallas kernels: none -> 208 us  [local(): pl.pallas_call(functools.partial(kernel, mem_count, reg_count, chunk, slo...]
    dot_general x48 -> x0, matrix products: 146 us -> none  [the longest x16 119 us: advance(): lax.dot_general(window_innov, tapered, (((1,), (1,)), ((), ())), preferre...]
    all_to_all x1 -> x0, blocking collectives: 109 us -> none  [local(): lax.all_to_all(result_cols.reshape(members, 1, per_dev * BLK), 'mem', spl...]
    ppermute x3 -> x0, waiting for transfers between devices: 88.2 us -> none  [from_behind(): return lax.ppermute(x, axis, [(i, (i + by) % size) for i in range(size)])]
    all_gather x1 -> x0, waiting for transfers between devices: 37.3 us -> none  [local(): lax.all_gather(stacked, 'mem', axis=1, tiled=True)]
    unnamed x19 -> x5, local copies, waits for them, and re-layouts: 41 us -> 3.82 us
    reshape x19 -> x0, local copies, waits for them, and re-layouts: 18.2 us -> none  [the longest x16 6.46 us: advance(): taper_tile = jnp.einsum('wt,tij->iwj', weights, tapers, precision=lax.Pre...]
    squeeze x1 -> x0, local copies, waits for them, and re-layouts: 8.55 us -> none  [local(): window_innov = window[1]]
  transfers between devices with their start and end apart: 5 -> 0, of which waited for: 2 -> 0; matrix products, arithmetic and copies ran while one was open for 5% -> 0% of each run, Pallas kernels for 0% -> 0%
where the time goes in v1:
time: 214 us
  Pallas kernels  208 us (97%)
  local copies, waits for them, and re-layouts  3.82 us (2%)
    pallas_call x1, Pallas kernels, local(): pl.pallas_call(functools.partial(kernel, mem_count, reg_count, chunk, slo...  208 us

profile of v1, /device:TPU:1, one launch (start us, length us, event | category | flops | bytes accessed | tf_op | source)
XLA Modules:
  0.0 213.7 jit_solution(5260221676382661065)
XLA Ops:
  0.0 0.8 dynamic-slice_add_fusion
  0.8 0.1 select_reduce_fusion.index_ref
  0.9 1.1 pad_multiply_fusion.taper_ref
  2.0 0.0 copy-start
  2.0 0.9 copy-done
  2.9 0.0 copy-start.1
  2.9 0.9 copy-done.1
  3.8 207.9 %shard_map.64 = bf16[128,16384]{1,0:T(8,128)(2,1)S(1)} custom-call(s32[16,20]{1,0:T(8,128)S(1)} %select_reduce_fusion.index_ref, f32[9,128,128]{2,1,0:T(8,128)S(1)} %pad_multiply_fusion.taper_ref, bf16[128,16384]{1,0:T(8,128)(2,1)} %anomalies.1, bf16[128,512]{1,0:T(8,128)(2,1)S(1)} %copy-done, bf16[128,512]{1,0:T(8,128)(2,1)S(1)} %copy-done.1), custom_call_target="tpu_custom_call" | custom-call | flops 17179869184 | bytes 16777216 | tf_op jit(solution)/shard_map/pallas_call | solution.py:228
  211.7 2.0 copy.10
Async XLA Ops:
  2.0 0.9 copy-start
  2.9 0.9 copy-start.1

commit v2 on v1

--- a/solution.py
+++ b/solution.py
@@ -24,13 +24,14 @@
     slots,
     steps,
     index_ref,
-    taper_ref,
+    tapers,
     anomalies,
     obs,
     innov,
     out,
     patches,
     window,
+    tiles,
     turned,
     weighted,
     results,
@@ -44,6 +45,7 @@
     pair_recv,
     plane_send,
     plane_recv,
+    tile_sem,
 ):
     mem = lax.axis_index("mem")
     reg = lax.axis_index("reg")
@@ -65,21 +67,14 @@
     def region(step):
         return lax.rem(reg + step + reg_count, reg_count)
 
+    load = pltpu.make_async_copy(tapers, tiles.at[pl.ds(1, tapers.shape[0])], tile_sem)
+    load.start()
     barrier = pltpu.get_barrier_semaphore()
     for by in range(1, mem_count):
         pl.semaphore_signal(barrier, inc=1, device_id=(device(by), reg), device_id_type=MESH)
     for step in steps:
         pl.semaphore_signal(barrier, inc=1, device_id=(mem, region(step)), device_id_type=MESH)
     pl.semaphore_wait(barrier, mem_count - 1 + len(steps))
-
-    for kind, shard in ((0, obs), (1, innov)):
-        there = window.at[home, kind, chip, core]
-        for by in range(1, chips):
-            peer = lax.rem(chip + by, chips) * CORES + core
-            pltpu.make_async_remote_copy(
-                shard, there, line_send, line_recv, device_id=(peer, reg), device_id_type=MESH
-            ).start()
-        pltpu.make_async_copy(shard, there, line_recv).start()
 
     def send_patches(c, carry):
         there = patches.at[c, mine]
@@ -98,9 +93,48 @@
         pltpu.make_async_copy(anomalies.at[:, pl.ds(first, chunk)], there, patch_recv.at[c]).start()
         return carry
 
-    early = max(1, chunks // 8)
-    middle = max(early, chunks * 5 // 8)
-    lax.fori_loop(0, early, send_patches, 0)
+    def flipped(mask):
+        at = chip
+        bit = 1
+        while bit < chips:
+            if mask & bit:
+                at = at + bit * (1 - 2 * lax.rem(at // bit, 2))
+            bit *= 2
+        return at
+
+    issued = 0
+    held = [0]
+    for kind, shard in ((0, obs), (1, innov)):
+        pltpu.make_async_copy(shard, window.at[home, kind, chip, core], line_recv.at[0]).start()
+    bit = chips // 2
+    while bit >= 1:
+        peer = flipped(bit) * CORES + core
+        for mask in held:
+            for kind, shard in ((0, obs), (1, innov)):
+                there = window.at[home, kind, flipped(mask), core]
+                pltpu.make_async_remote_copy(
+                    there if mask else shard,
+                    there,
+                    line_send,
+                    line_recv.at[mask + bit],
+                    device_id=(peer, reg),
+                    device_id_type=MESH,
+                ).start()
+        if issued < chunks:
+            send_patches(issued, 0)
+            issued += 1
+        if bit == chips // 2:
+            load.wait()
+            tiles[0] = jnp.zeros_like(tiles[0])
+            for t in range(tapers.shape[0]):
+                tiles[t + 1] = tiles[t + 1] / (mem_count * mem_dev - 1)
+        came = [mask + bit for mask in held]
+        for mask in came:
+            wait_for(window.at[home, :, flipped(mask), core], line_recv.at[mask])
+        held = held + came
+        bit //= 2
+    wait_for(window.at[home, :, chip, core], line_recv.at[0])
+    middle = max(issued, chunks * 5 // 8)
 
     def share(slot):
         return window.at[slot, :, :, core]
@@ -118,7 +152,6 @@
             device_id_type=MESH,
         ).start()
 
-    wait_for(share(home), line_recv)
     for step in steps:
         slot = (REACH - step) % reg_count
         pltpu.make_async_remote_copy(
@@ -130,7 +163,7 @@
             device_id_type=MESH,
         ).start()
     to_twin(home)
-    lax.fori_loop(early, middle, send_patches, 0)
+    lax.fori_loop(issued, middle, send_patches, 0)
     for step in steps:
         slot = (REACH - step) % reg_count
         wait_for(share(slot), plane_recv.at[slot])
@@ -156,7 +189,7 @@
                 for group in range(groups):
                     tile = None
                     for w in range(slot * groups + group, positions, reg_count * groups):
-                        one = taper_ref[index_ref[c * (chunk // BLK) + part, w]]
+                        one = tiles[index_ref[c * (chunk // BLK) + part, w]]
                         tile = one if tile is None else tile + one
                     piece = cov[part * BLK : (part + 1) * BLK, group * BLK : (group + 1) * BLK]
                     weighted[
@@ -222,7 +255,6 @@
     position_ids = jnp.arange(positions, dtype=jnp.int32)
     linked = my_links[:, :, None] == position_ids[None, None, :]
     index = jnp.sum(jnp.where(linked, my_choice[:, :, None] + 1, 0), axis=1).astype(jnp.int32)
-    tiles = jnp.concatenate([jnp.zeros((1, BLK, BLK), jnp.float32), tapers]) / (members - 1)
     DMA = pltpu.SemaphoreType.DMA
     chips = mem_count // CORES
     return pl.pallas_call(
@@ -230,15 +262,16 @@
         out_shape=jax.ShapeDtypeStruct((mem_dev, state_cols), jnp.bfloat16),
         in_specs=[
             pl.BlockSpec(memory_space=pltpu.SMEM),
-            pl.BlockSpec(memory_space=pltpu.VMEM),
-            pl.BlockSpec(memory_space=pl.ANY),
-            pl.BlockSpec(memory_space=pl.ANY),
-            pl.BlockSpec(memory_space=pl.ANY),
+            pl.BlockSpec(memory_space=pltpu.HBM),
+            pl.BlockSpec(memory_space=pltpu.HBM),
+            pl.BlockSpec(memory_space=pltpu.HBM),
+            pl.BlockSpec(memory_space=pltpu.HBM),
         ],
         out_specs=pl.BlockSpec(memory_space=pl.ANY),
         scratch_shapes=[
             pltpu.VMEM((chunks, members, chunk), jnp.bfloat16),
             pltpu.VMEM((slots, 2, chips, CORES, mem_dev, obs_cols), jnp.bfloat16),
+            pltpu.VMEM((tapers.shape[0] + 1, BLK, BLK), jnp.float32),
             pltpu.VMEM((chunk, members), jnp.bfloat16),
             pltpu.VMEM((slots, chunk, obs_cols), jnp.bfloat16),
             pltpu.VMEM((chunks, members, chunk), jnp.bfloat16),
@@ -247,21 +280,22 @@
             DMA,
             DMA,
             DMA,
-            DMA,
+            DMA((chips,)),
             DMA((slots,)),
             DMA((slots,)),
             DMA((slots,)),
             DMA((slots,)),
+            DMA,
         ],
         compiler_params=pltpu.CompilerParams(
-            collective_id=0, has_side_effects=True, vmem_limit_bytes=48 * 1024 * 1024
+            collective_id=0, has_side_effects=True, vmem_limit_bytes=56 * 1024 * 1024
         ),
         cost_estimate=pl.CostEstimate(
             flops=4 * members * per_dev * BLK * slots * obs_cols,
             bytes_accessed=4 * mem_dev * state_cols * 2,
             transcendentals=0,
         ),
-    )(index, tiles, anomalies, obs_anomalies, innovations)
+    )(index, tapers, anomalies, obs_anomalies, innovations)
 
 
 def solution(mesh):

time: 214 us -> 214 us (level)
    unnamed x5 -> x1, local copies, waits for them, and re-layouts: 3.82 us -> 4.57 us
where the time goes in v2:
time: 214 us; the launch traced here: 213 us
  Pallas kernels  207 us (97%)
  local copies, waits for them, and re-layouts  4.57 us (2%)
    pallas_call x1, Pallas kernels, local(): pl.pallas_call(functools.partial(kernel, mem_count, reg_count, chunk, slo...  207 us
    unnamed x1, local copies, waits for them, and re-layouts  4.57 us

profile of v2, /device:TPU:1, one launch (start us, length us, event | category | flops | bytes accessed | tf_op | source)
XLA Modules:
  0.0 213.4 jit_solution(9495796201214044622)
XLA Ops:
  0.0 0.8 dynamic-slice_add_fusion
  0.8 0.7 select_reduce_fusion.index_ref
  1.5 207.3 %shard_map.64 = bf16[128,16384]{1,0:T(8,128)(2,1)} custom-call(s32[16,20]{1,0:T(8,128)} %select_reduce_fusion.index_ref, f32[8,128,128]{2,1,0:T(8,128)} %tapers.1, bf16[128,16384]{1,0:T(8,128)(2,1)} %anomalies.1, bf16[128,512]{1,0:T(8,128)(2,1)} %obs.1, bf16[128,512]{1,0:T(8,128)(2,1)} %innov.1), custom_call_target="tpu_custom_call" | custom-call | flops 17179869184 | bytes 16777216 | tf_op jit(solution)/shard_map/pallas_call | solution.py:260
  208.8 4.6 %copy.10 = bf16[128,16384]{1,0:T(8,128)(2,1)} copy(bf16[128,16384]{1,0:T(8,128)(2,1)} %shard_map.64) | data formatting | bytes 8388608

commit v3 on v2

--- a/solution.py
+++ b/solution.py
@@ -102,8 +102,28 @@
             bit *= 2
         return at
 
+    def to_plane(mask):
+        for step in steps:
+            slot = (REACH - step) % reg_count
+            if mask:
+                pieces = [window.at[home, :, flipped(mask), core]]
+                places = [window.at[slot, :, flipped(mask), core]]
+            else:
+                pieces = [obs, innov]
+                places = [window.at[slot, kind, chip, core] for kind in (0, 1)]
+            for piece, place in zip(pieces, places):
+                pltpu.make_async_remote_copy(
+                    piece,
+                    place,
+                    plane_send.at[slot],
+                    plane_recv.at[slot],
+                    device_id=(mem, region(step)),
+                    device_id_type=MESH,
+                ).start()
+
     issued = 0
     held = [0]
+    fresh = [0]
     for kind, shard in ((0, obs), (1, innov)):
         pltpu.make_async_copy(shard, window.at[home, kind, chip, core], line_recv.at[0]).start()
     bit = chips // 2
@@ -120,6 +140,8 @@
                     device_id=(peer, reg),
                     device_id_type=MESH,
                 ).start()
+        for mask in fresh:
+            to_plane(mask)
         if issued < chunks:
             send_patches(issued, 0)
             issued += 1
@@ -132,9 +154,12 @@
         for mask in came:
             wait_for(window.at[home, :, flipped(mask), core], line_recv.at[mask])
         held = held + came
+        fresh = came
         bit //= 2
     wait_for(window.at[home, :, chip, core], line_recv.at[0])
-    middle = max(issued, chunks * 5 // 8)
+    for mask in fresh:
+        to_plane(mask)
+    middle = max(issued, chunks * 6 // 8)
 
     def share(slot):
         return window.at[slot, :, :, core]
@@ -152,16 +177,6 @@
             device_id_type=MESH,
         ).start()
 
-    for step in steps:
-        slot = (REACH - step) % reg_count
-        pltpu.make_async_remote_copy(
-            share(home),
-            share(slot),
-            plane_send.at[slot],
-            plane_recv.at[slot],
-            device_id=(mem, region(step)),
-            device_id_type=MESH,
-        ).start()
     to_twin(home)
     lax.fori_loop(issued, middle, send_patches, 0)
     for step in steps:

time: 214 us -> 206 us (0.963)
  Pallas kernels: 207 us -> 199 us
    pallas_call x1, Pallas kernels: 207 us -> 199 us  [local(): pl.pallas_call(functools.partial(kernel, mem_count, reg_count, chunk, slo...]
where the time goes in v3:
time: 206 us; the launch traced here: 205 us
  Pallas kernels  199 us (97%)
  local copies, waits for them, and re-layouts  4.57 us (2%)
    pallas_call x1, Pallas kernels, local(): pl.pallas_call(functools.partial(kernel, mem_count, reg_count, chunk, slo...  199 us
    unnamed x1, local copies, waits for them, and re-layouts  4.57 us

profile of v3, /device:TPU:1, one launch (start us, length us, event | category | flops | bytes accessed | tf_op | source)
XLA Modules:
  0.0 205.5 jit_solution(12990468415595591578)
XLA Ops:
  0.0 0.8 dynamic-slice_add_fusion
  0.8 0.7 select_reduce_fusion.index_ref
  1.5 199.4 %shard_map.64 = bf16[128,16384]{1,0:T(8,128)(2,1)} custom-call(s32[16,20]{1,0:T(8,128)} %select_reduce_fusion.index_ref, f32[8,128,128]{2,1,0:T(8,128)} %tapers.1, bf16[128,16384]{1,0:T(8,128)(2,1)} %anomalies.1, bf16[128,512]{1,0:T(8,128)(2,1)} %obs.1, bf16[128,512]{1,0:T(8,128)(2,1)} %innov.1), custom_call_target="tpu_custom_call" | custom-call | flops 17179869184 | bytes 16777216 | tf_op jit(solution)/shard_map/pallas_call | solution.py:275
  200.9 4.6 %copy.10 = bf16[128,16384]{1,0:T(8,128)(2,1)} copy(bf16[128,16384]{1,0:T(8,128)(2,1)} %shard_map.64) | data formatting | bytes 8388608

commit v4 on v3

--- a/solution.py
+++ b/solution.py
@@ -102,9 +102,27 @@
             bit *= 2
         return at
 
+    relay = reg_count == 4
+    if relay:
+        across = {1: reg + 1 - 2 * lax.rem(reg, 2), 2: lax.rem(reg + 2, 4), 3: 3 - reg}
+
+        def slot_at(receiver, source):
+            return lax.rem(source - receiver + REACH + 4, 4)
+
+        lanes = [
+            (key, across[key], slot_at(across[key], reg), slot_at(reg, across[key]))
+            for key in (1, 2)
+        ]
+        home_key = 0
+    else:
+        lanes = [
+            ((REACH - step) % reg_count, region(step), (REACH - step) % reg_count, (REACH - step) % reg_count)
+            for step in steps
+        ]
+        home_key = home
+
     def to_plane(mask):
-        for step in steps:
-            slot = (REACH - step) % reg_count
+        for key, there, slot, _ in lanes:
             if mask:
                 pieces = [window.at[home, :, flipped(mask), core]]
                 places = [window.at[slot, :, flipped(mask), core]]
@@ -115,9 +133,9 @@
                 pltpu.make_async_remote_copy(
                     piece,
                     place,
-                    plane_send.at[slot],
-                    plane_recv.at[slot],
-                    device_id=(mem, region(step)),
+                    plane_send.at[key],
+                    plane_recv.at[key],
+                    device_id=(mem, there),
                     device_id_type=MESH,
                 ).start()
 
@@ -167,28 +185,42 @@
     def other(slot):
         return window.at[slot, :, :, 1 - core]
 
-    def to_twin(slot):
+    def to_twin(slot, key):
         pltpu.make_async_remote_copy(
             share(slot),
             share(slot),
-            pair_send.at[slot],
-            pair_recv.at[slot],
+            pair_send.at[key],
+            pair_recv.at[key],
             device_id=(twin, reg),
             device_id_type=MESH,
         ).start()
 
-    to_twin(home)
+    to_twin(home, home_key)
     lax.fori_loop(issued, middle, send_patches, 0)
-    for step in steps:
-        slot = (REACH - step) % reg_count
-        wait_for(share(slot), plane_recv.at[slot])
-        to_twin(slot)
+    for key, _, _, slot in lanes:
+        wait_for(share(slot), plane_recv.at[key])
+        if relay:
+            onward, kind = 3 - key, 2 - key
+            pltpu.make_async_remote_copy(
+                window.at[slot, kind, :, core],
+                window.at[slot_at(across[onward], across[key]), kind, :, core],
+                plane_send.at[3],
+                plane_recv.at[3],
+                device_id=(mem, across[onward]),
+                device_id_type=MESH,
+            ).start()
+        to_twin(slot, key)
     lax.fori_loop(middle, chunks, send_patches, 0)
-    for slot in range(slots):
-        wait_for(other(slot), pair_recv.at[slot])
+    arrivals = [(home_key, home)] + [(key, slot) for key, _, _, slot in lanes]
+    if relay:
+        opposite = slot_at(reg, across[3])
+        wait_for(share(opposite), plane_recv.at[3])
+        to_twin(opposite, 3)
+        arrivals.append((3, opposite))
+    for key, slot in arrivals:
+        wait_for(other(slot), pair_recv.at[key])
 
     members = mem_count * mem_dev
-    rows = min(256, members)
     positions = (2 * REACH + 1) * groups
 
     def analyse(c, carry):
@@ -244,10 +276,10 @@
     wait_for(anomalies.at[:, sent], patch_send)
     wait_for(out.at[:, sent], out_send)
     wait_for(window.at[home, :, 0 : chips - 1, 0], line_send)
-    for slot in range(slots):
-        wait_for(share(slot), pair_send.at[slot])
-        if slot != home:
-            wait_for(share(home), plane_send.at[slot])
+    for key, _ in arrivals:
+        wait_for(share(home), pair_send.at[key])
+        if key != home_key:
+            wait_for(share(home), plane_send.at[key])
 
 
 def local(anomalies, obs_anomalies, innovations, obs_links, taper_choice, tapers):

time: 206 us -> 206 us (level)
  no operation moved by 1% of the time
where the time goes in v4:
time: 206 us; the launch traced here: 205 us
  Pallas kernels  199 us (97%)
  local copies, waits for them, and re-layouts  4.57 us (2%)
    pallas_call x1, Pallas kernels, local(): pl.pallas_call(functools.partial(kernel, mem_count, reg_count, chunk, slo...  199 us
    unnamed x1, local copies, waits for them, and re-layouts  4.57 us

profile of v4, /device:TPU:1, one launch (start us, length us, event | category | flops | bytes accessed | tf_op | source)
XLA Modules:
  0.0 205.5 jit_solution(18038232878447938433)
XLA Ops:
  0.0 0.8 dynamic-slice_add_fusion
  0.8 0.7 select_reduce_fusion.index_ref
  1.5 199.4 %shard_map.64 = bf16[128,16384]{1,0:T(8,128)(2,1)} custom-call(s32[16,20]{1,0:T(8,128)} %select_reduce_fusion.index_ref, f32[8,128,128]{2,1,0:T(8,128)} %tapers.1, bf16[128,16384]{1,0:T(8,128)(2,1)} %anomalies.1, bf16[128,512]{1,0:T(8,128)(2,1)} %obs.1, bf16[128,512]{1,0:T(8,128)(2,1)} %innov.1), custom_call_target="tpu_custom_call" | custom-call | flops 17179869184 | bytes 16777216 | tf_op jit(solution)/shard_map/pallas_call | solution.py:307
  200.9 4.6 %copy.10 = bf16[128,16384]{1,0:T(8,128)(2,1)} copy(bf16[128,16384]{1,0:T(8,128)(2,1)} %shard_map.64) | data formatting | bytes 8388608

commit v5 on v3

--- a/solution.py
+++ b/solution.py
@@ -23,7 +23,8 @@
     chunk,
     slots,
     steps,
-    index_ref,
+    links,
+    choice,
     tapers,
     anomalies,
     obs,
@@ -46,6 +47,7 @@
     plane_send,
     plane_recv,
     tile_sem,
+    index_ref,
 ):
     mem = lax.axis_index("mem")
     reg = lax.axis_index("reg")
@@ -179,6 +181,20 @@
 
     to_twin(home)
     lax.fori_loop(issued, middle, send_patches, 0)
+    per_dev = own_cols // BLK
+
+    def list_tiles(b, carry):
+        row = mem * per_dev + b
+        at = [links[k, row] for k in range(links.shape[0])]
+        tile = [choice[k, row] + 1 for k in range(links.shape[0])]
+        for w in range((2 * REACH + 1) * groups):
+            found = jnp.int32(0)
+            for a, t in zip(at, tile):
+                found = jnp.where(a == w, t, found)
+            index_ref[b, w] = found
+        return carry
+
+    lax.fori_loop(0, per_dev, list_tiles, 0)
     for step in steps:
         slot = (REACH - step) % reg_count
         wait_for(share(slot), plane_recv.at[slot])
@@ -264,18 +280,13 @@
     slots = min(2 * REACH + 1, reg_count)
     home = REACH % reg_count
     steps = [(REACH - slot) for slot in range(slots) if slot != home]
-    first_block = lax.axis_index("mem") * per_dev
-    my_links = lax.dynamic_slice_in_dim(obs_links, first_block, per_dev, 0)
-    my_choice = lax.dynamic_slice_in_dim(taper_choice, first_block, per_dev, 0)
-    position_ids = jnp.arange(positions, dtype=jnp.int32)
-    linked = my_links[:, :, None] == position_ids[None, None, :]
-    index = jnp.sum(jnp.where(linked, my_choice[:, :, None] + 1, 0), axis=1).astype(jnp.int32)
     DMA = pltpu.SemaphoreType.DMA
     chips = mem_count // CORES
     return pl.pallas_call(
         functools.partial(kernel, mem_count, reg_count, chunk, slots, steps),
         out_shape=jax.ShapeDtypeStruct((mem_dev, state_cols), jnp.bfloat16),
         in_specs=[
+            pl.BlockSpec(memory_space=pltpu.SMEM),
             pl.BlockSpec(memory_space=pltpu.SMEM),
             pl.BlockSpec(memory_space=pltpu.HBM),
             pl.BlockSpec(memory_space=pltpu.HBM),
@@ -301,6 +312,7 @@
             DMA((slots,)),
             DMA((slots,)),
             DMA,
+            pltpu.SMEM((per_dev, positions), jnp.int32),
         ],
         compiler_params=pltpu.CompilerParams(
             collective_id=0, has_side_effects=True, vmem_limit_bytes=56 * 1024 * 1024
@@ -310,7 +322,7 @@
             bytes_accessed=4 * mem_dev * state_cols * 2,
             transcendentals=0,
         ),
-    )(index, tapers, anomalies, obs_anomalies, innovations)
+    )(obs_links.T, taper_choice.T, tapers, anomalies, obs_anomalies, innovations)
 
 
 def solution(mesh):

time: 206 us -> 204 us (level)
  no operation moved by 1% of the time
where the time goes in v5:
time: 204 us
  Pallas kernels  200 us (98%)
  local copies, waits for them, and re-layouts  4.57 us (2%)
    pallas_call x1, Pallas kernels, local(): pl.pallas_call(functools.partial(kernel, mem_count, reg_count, chunk, slo...  200 us
    unnamed x1, local copies, waits for them, and re-layouts  4.57 us

profile of v5, /device:TPU:1, one launch (start us, length us, event | category | flops | bytes accessed | tf_op | source)
XLA Modules:
  0.0 204.1 jit_solution(5118922895476563929)
XLA Ops:
  0.0 199.5 %shard_map.64 = bf16[128,16384]{1,0:T(8,128)(2,1)} custom-call(s32[12,128]{1,0:T(8,128)} %bitcast.2, s32[12,128]{1,0:T(8,128)} %bitcast.3, f32[8,128,128]{2,1,0:T(8,128)} %tapers.1, bf16[128,16384]{1,0:T(8,128)(2,1)} %anomalies.1, bf16[128,512]{1,0:T(8,128)(2,1)} %obs.1, bf16[128,512]{1,0:T(8,128)(2,1)} %innov.1), custom_call_target="tpu_custom_call" | custom-call | flops 17179869184 | bytes 16777216 | tf_op jit(solution)/shard_map/pallas_call | solution.py:285
  199.5 4.6 %copy.8 = bf16[128,16384]{1,0:T(8,128)(2,1)} copy(bf16[128,16384]{1,0:T(8,128)(2,1)} %shard_map.64) | data formatting | bytes 8388608
